TPU v7x, 32 devices: a whole 2x2x4 slice. The times are simulated.
32 devices in a mesh: tm: 4 (over x, core), tile: 8 (over z, y).
Axes of the slice: x: 2, y: 2, z: 4, core: 2. Of those that a mesh axis runs over, the one named last changes fastest.
Arguments:
- latents: bfloat16 [8, 160, 16, 16], P('tm', 'tile'), may hold values from -6 to 6
- w_in: bfloat16 [3, 3, 3, 16, 384], replicated, may hold values from -0.3125 to 0.3125
- b_in: bfloat16 [384], replicated, may hold values from -3 to 3
- w_up: bfloat16 [3, 3, 384, 192], replicated, may hold values from -0.109375 to 0.109375
- b_up: bfloat16 [192], replicated, may hold values from -3 to 3
- gain_one: bfloat16 [192], replicated, may hold values from 0.099609375 to 1.8984375
- w_one: bfloat16 [3, 3, 3, 192, 192], replicated, may hold values from -0.078125 to 0.078125
- b_one: bfloat16 [192], replicated, may hold values from -3 to 3
- gain_two: bfloat16 [192], replicated, may hold values from 0.099609375 to 1.8984375
- w_two: bfloat16 [3, 3, 3, 192, 192], replicated, may hold values from -0.078125 to 0.078125
- b_two: bfloat16 [192], replicated, may hold values from -3 to 3
Outputs:
- decoded: bfloat16 [8, 32, 320, 192], P('tm', 'tile')
All inputs are finite; a program needn't handle non-finite values.
Results may differ from a plain program's by a relative error of at most 0.0095.
Values may be sent and summed in bfloat16 or wider, within the bound.
A program may use at most 64 MiB of HBM per device.

v0:
```python
import functools

import jax
import jax.numpy as jnp
from jax import lax
from jax.experimental import pallas as pl
from jax.experimental.pallas import tpu as pltpu
from jax.sharding import PartitionSpec as P

MESH = pl.DeviceIdType.MESH
F32 = jnp.float32
BF16 = jnp.bfloat16


def dot(a, b):
    return jnp.dot(a, b, preferred_element_type=F32)


def activate(v, gain):
    v = v.astype(F32)
    inv = lax.rsqrt(jnp.mean(v * v, axis=-1, keepdims=True) + 1e-6)
    half = 0.5 * (v * inv * gain)
    return half + half * jnp.tanh(half)


def after(v):
    rolled = pltpu.roll(v, 1, 0)
    return jnp.where(lax.broadcasted_iota(jnp.int32, v.shape, 0) == 0, 0.0, rolled)


def ahead(v):
    n = v.shape[0]
    rolled = pltpu.roll(v, n - 1, 0)
    return jnp.where(lax.broadcasted_iota(jnp.int32, v.shape, 0) == n - 1, 0.0, rolled)


def kernel(ntm, nt, height, shard, zch,
           lat, w_in, b_in, w_up, b_up, g_one, w_one, b_one, g_two, w_two, b_two,
           out,
           lbuf, lf32, sel, cols, first, wc, plane, a1, a2, acc,
           lsend, lrecv, osend, hsend, arecv):
    tm = lax.axis_index("tm")
    tile = lax.axis_index("tile")
    ncol = nt * shard
    dim = first.shape[-1]
    upd = plane.shape[-1]

    barrier = pltpu.get_barrier_semaphore()

    def others(d, body):
        def step(k, c):
            body(lax.rem(tile + k, nt))
            return c
        lax.fori_loop(1 if d == 0 else 0, nt, step, 0)

    for d in range(3):
        @pl.when(tm - d >= 0)
        def _():
            others(d, lambda s: pl.semaphore_signal(
                barrier, inc=1, device_id=(tm - d, s), device_id_type=MESH))
    pl.semaphore_wait(barrier, nt * jnp.minimum(3, ntm - tm) - 1)

    def send_lat(d, s):
        return pltpu.make_async_remote_copy(
            src_ref=lat, dst_ref=lbuf.at[d, tile], send_sem=lsend.at[d, s],
            recv_sem=lrecv.at[d, tile], device_id=(tm + d, s), device_id_type=MESH)

    for d in (2, 1, 0):
        @pl.when(tm + d < ntm)
        def _():
            others(d, lambda s: send_lat(d, s).start())

    lbuf[0, tile] = lat[...]
    for d in (1, 2):
        @pl.when(tm - d < 0)
        def _():
            lbuf[d] = jnp.zeros(lbuf.shape[1:], BF16)

    wide = height * zch
    for r in range(4):
        k = lax.broadcasted_iota(jnp.int32, (wide, 256), 0)
        n = lax.broadcasted_iota(jnp.int32, (wide, 256), 1)
        krow, kch = k // zch, k % zch
        p, ch = n // (3 * zch), n % zch
        hit = (krow == 2 * tile - 2 + r + p) & (kch == ch) & (n < 9 * zch)
        sel[:, 256 * r:256 * r + 256] = jnp.where(hit, 1.0, 0.0).astype(BF16)

    def phases(j, c):
        at = pl.ds(pl.multiple_of(j * 64, 64), 64)
        w = [[w_up[3 * p + q, at].astype(F32) for q in range(3)] for p in range(3)]

        def joined(v, phase):
            if phase == 0:
                return [v[0], v[1] + v[2]]
            return [v[0] + v[1], v[2]]

        for a in range(2):
            rows = [joined([w[p][q] for p in range(3)], a) for q in range(3)]
            for b in range(2):
                for rr in range(2):
                    both = joined([rows[q][rr] for q in range(3)], b)
                    for cc in range(2):
                        wc[2 * a + b, 2 * rr + cc, at] = both[cc].astype(BF16)
        return c
    lax.fori_loop(0, dim // 64, phases, 0)

    for d in range(3):
        @pl.when(tm - d >= 0)
        def _():
            def arrived(s):
                pltpu.make_async_remote_copy(
                    src_ref=lat, dst_ref=lbuf.at[d, s], send_sem=lsend.at[d, s],
                    recv_sem=lrecv.at[d, s], device_id=(tm, s), device_id_type=MESH).wait_recv()
            others(d, arrived)

    for d in range(3):
        for s in range(nt):
            v = lbuf[d, s].astype(F32)
            for f in range(2):
                lf32[2 * (2 - d) + f, s * shard:(s + 1) * shard] = v[f * shard:(f + 1) * shard]

    def gather(f, c):
        raw = lf32[f].astype(BF16)
        for r in range(4):
            z = dot(raw, sel[:, 256 * r:256 * r + 256])
            q = lax.broadcasted_iota(jnp.int32, z.shape, 1) % (3 * zch) // zch
            z = jnp.where(q == 0, after(z), jnp.where(q == 2, ahead(z), z))
            cols[f, r] = z.astype(BF16)
        return c
    lax.fori_loop(0, 6, gather, 0)

    def conv_in(k, c):
        f, r = k // 4, k % 4
        v = b_in[...] + sum(dot(cols[f + a, r][:, :9 * zch], w_in[a]) for a in range(3))
        row = 2 * tile - 1 + r
        keep = ((row >= 0) & (row < height)).astype(F32)
        v = v * keep
        first[0, f, r] = after(v).astype(BF16)
        first[1, f, r] = v.astype(BF16)
        first[2, f, r] = ahead(v).astype(BF16)
        return c
    lax.fori_loop(0, 16, conv_in, 0)

    def split_store(ref, at, b, v):
        if b == 0:
            ref[at[0], at[1], ncol:2 * ncol] = v.astype(BF16)
            ref[at[0], at[1], 3 * ncol:] = ahead(v).astype(BF16)
        else:
            ref[at[0], at[1], 2 * ncol:3 * ncol] = v.astype(BF16)
            ref[at[0], at[1], :ncol] = after(v).astype(BF16)

    def conv_up(f, c):
        seen = ((tm > 0) | (f >= 2))
        for a in range(2):
            for b in range(2):
                v = b_up[...]
                for rr in range(2):
                    for cc in range(2):
                        x = first[b + cc, f, rr:rr + 3].reshape(3 * ncol, dim)
                        v = v + dot(x, wc[2 * a + b, 2 * rr + cc])
                v = v.astype(BF16)
                for base in range(3):
                    row = 2 * base + 1 - a
                    here = v[base * ncol:(base + 1) * ncol]
                    plane[f, row, b * ncol:(b + 1) * ncol] = here
                    ok = seen
                    if row == 0:
                        ok = ok & (tile > 0)
                    if row == 5:
                        ok = ok & (tile < nt - 1)
                    split_store(a1, (f, row), b, activate(here, g_one[...]) * ok.astype(F32))
        return c
    lax.fori_loop(0, 4, conv_up, 0)

    def conv_part(ref, w, f, r, kts):
        total = None
        for kt in kts:
            for kh in range(3):
                for kw in range(3):
                    x = ref[f + kt, r + kh, kw * ncol:(kw + 2) * ncol]
                    term = dot(x, w[9 * kt + 3 * kh + kw])
                    total = term if total is None else total + term
        return total

    centre = pl.ds(ncol, 2 * ncol)

    def copy(f, row, to_f, to_row, dtm, dtile, send):
        return pltpu.make_async_remote_copy(
            src_ref=a2.at[f, row, centre], dst_ref=a2.at[to_f, to_row, centre], send_sem=send,
            recv_sem=arecv.at[to_f, to_row], device_id=(tm + dtm, tile + dtile),
            device_id_type=MESH)

    def sends(f, r, act):
        @pl.when(tm + 1 < ntm)
        def _():
            act(copy(f + 2, r + 1, f, r + 1, 1, 0, osend.at[f, r]))

        @pl.when((r == 0) & (tile > 0))
        def _():
            act(copy(f + 2, r + 1, f + 2, 5, 0, -1, hsend.at[f, 0, 0]))

        @pl.when((r == 0) & (tile > 0) & (tm + 1 < ntm))
        def _():
            act(copy(f + 2, r + 1, f, 5, 1, -1, hsend.at[f, 0, 1]))

        @pl.when((r == 3) & (tile < nt - 1))
        def _():
            act(copy(f + 2, r + 1, f + 2, 0, 0, 1, hsend.at[f, 1, 0]))

        @pl.when((r == 3) & (tile < nt - 1) & (tm + 1 < ntm))
        def _():
            act(copy(f + 2, r + 1, f, 0, 1, 1, hsend.at[f, 1, 1]))

    def where_at(k):
        f = k % 2
        h = k // 2
        return f, jnp.where(h == 0, 0, jnp.where(h == 1, 3, h - 1))

    def conv_mid(k, c):
        f, r = where_at(k)
        v = (conv_part(a1, w_one, f, r, (0, 1, 2)) + b_one[...]).astype(BF16)
        v = activate(v, g_two[...])
        split_store(a2, (f + 2, r + 1), 0, v[:ncol])
        split_store(a2, (f + 2, r + 1), 1, v[ncol:])
        sends(f, r, lambda c: c.start())
        return c
    lax.fori_loop(0, 8, conv_mid, 0)

    def receive(f, row, ok):
        @pl.when(ok)
        def _():
            copy(f, row, f, row, 0, 0, osend.at[0, 0]).wait_recv()
            a2[f, row, 3 * ncol:] = ahead(a2[f, row, ncol:2 * ncol].astype(F32)).astype(BF16)
            a2[f, row, :ncol] = after(a2[f, row, 2 * ncol:3 * ncol].astype(F32)).astype(BF16)

        @pl.when(jnp.logical_not(ok))
        def _():
            a2[f, row] = jnp.zeros(a2.shape[2:], BF16)

    for f in (2, 3):
        receive(f, 0, tile > 0)
        receive(f, 5, tile < nt - 1)

    def conv_near(r, c):
        acc[0, r] = conv_part(a2, w_two, 0, r, (2,))
        acc[1, r] = conv_part(a2, w_two, 1, r, (1, 2))
        return c
    lax.fori_loop(0, 4, conv_near, 0)

    for f in (0, 1):
        receive(f, 0, (tm > 0) & (tile > 0))
        receive(f, 5, (tm > 0) & (tile < nt - 1))

        def middle_rows(row, c):
            receive(f, row, tm > 0)
            return c
        lax.fori_loop(1, 5, middle_rows, 0)

    m = lax.broadcasted_iota(jnp.int32, (2 * ncol, 2 * ncol), 0)
    n = lax.broadcasted_iota(jnp.int32, (2 * ncol, 2 * ncol), 1)
    weave = jnp.where(n == (m % 2) * ncol + m // 2, 1.0, 0.0).astype(BF16)

    def conv_far(r, c):
        for f, kts in ((0, (0, 1)), (1, (0,))):
            v = acc[f, r] + conv_part(a2, w_two, f, r, kts) + b_two[...]
            v = (v + plane[f + 2, r + 1].astype(F32)).astype(BF16)
            out[f, r] = dot(weave, v).astype(BF16)
        return c
    lax.fori_loop(0, 4, conv_far, 0)

    for d in range(3):
        @pl.when(tm + d < ntm)
        def _():
            others(d, lambda s: send_lat(d, s).wait_send())

    def left(k, c):
        f, r = where_at(k)
        sends(f, r, lambda c: c.wait_send())
        return c
    lax.fori_loop(0, 8, left, 0)


def per_device(latents, w_in, b_in, w_up, b_up, gain_one, w_one, b_one, gain_two, w_two, b_two):
    ntm, nt = lax.axis_size("tm"), lax.axis_size("tile")
    frames, shard, height, zch = latents.shape
    dim, upd = w_up.shape[2:]
    ncol = nt * shard
    lat = latents.reshape(frames * shard, height * zch)
    deep = -(-frames * shard // 16) * 16
    lat = jnp.pad(lat, ((0, deep - frames * shard), (0, 0)))
    wide = height * zch
    vec = lambda v: v.astype(F32).reshape(1, -1)
    args = (lat, w_in.reshape(3, 9 * zch, dim), vec(b_in), w_up.reshape(9, dim, upd), vec(b_up),
            vec(gain_one), w_one.reshape(27, upd, upd), vec(b_one), vec(gain_two),
            w_two.reshape(27, upd, upd), vec(b_two))
    vmem = pl.BlockSpec(memory_space=pltpu.VMEM)
    dma = pltpu.SemaphoreType.DMA
    return pl.pallas_call(
        functools.partial(kernel, ntm, nt, height, shard, zch),
        out_shape=jax.ShapeDtypeStruct((frames, 4, 2 * ncol, upd), BF16),
        in_specs=[vmem] * len(args),
        out_specs=vmem,
        scratch_shapes=[
            pltpu.VMEM((3, nt, deep, wide), BF16),
            pltpu.VMEM((6, ncol, wide), F32),
            pltpu.VMEM((wide, 1024), BF16),
            pltpu.VMEM((6, 4, ncol, 256), BF16),
            pltpu.VMEM((3, 4, 4, ncol, dim), BF16),
            pltpu.VMEM((4, 4, dim, upd), BF16),
            pltpu.VMEM((4, 6, 2 * ncol, upd), BF16),
            pltpu.VMEM((4, 6, 4 * ncol, upd), BF16),
            pltpu.VMEM((4, 6, 4 * ncol, upd), BF16),
            pltpu.VMEM((2, 4, 2 * ncol, upd), F32),
            dma((3, nt)),
            dma((3, nt)),
            dma((2, 4)),
            dma((2, 2, 2)),
            dma((4, 6)),
        ],
        compiler_params=pltpu.CompilerParams(
            collective_id=0, has_side_effects=True, vmem_limit_bytes=60 * 2**20),
    )(*args)


def solution(mesh):
    placed = (P("tm", "tile", None, None),) + (P(),) * 10
    return jax.shard_map(
        per_device,
        mesh=mesh,
        in_specs=placed,
        out_specs=P("tm", "tile", None, None),
        check_vma=False,
    )
```

profile of v0, /device:TPU:8, one launch (start us, length us, event | category | flops | bytes accessed | tf_op | source)
XLA Modules:
  0.0 98.4 jit_solution(606953801610509422)
XLA Ops:
  0.0 1.2 %reshape.64 = f32[192]{0:T(256)} convert(bf16[192]{0:T(256)(128)(2,1)} %param.15) | non-fusion elementwise | flops 192 | bytes 1152 | tf_op jit(solution)/shard_map/reshape | solution.py:292
  1.2 1.2 %reshape.66 = f32[192]{0:T(256)} convert(bf16[192]{0:T(256)(128)(2,1)} %param.16) | non-fusion elementwise | flops 192 | bytes 1152 | tf_op jit(solution)/shard_map/reshape | solution.py:292
  2.5 1.2 %reshape.68 = f32[192]{0:T(256)} convert(bf16[192]{0:T(256)(128)(2,1)} %param.18) | non-fusion elementwise | flops 192 | bytes 1152 | tf_op jit(solution)/shard_map/reshape | solution.py:292
  3.7 1.2 %reshape.70 = f32[192]{0:T(256)} convert(bf16[192]{0:T(256)(128)(2,1)} %param.19) | non-fusion elementwise | flops 192 | bytes 1152 | tf_op jit(solution)/shard_map/reshape | solution.py:292
  5.0 1.2 %reshape.72 = f32[192]{0:T(256)} convert(bf16[192]{0:T(256)(128)(2,1)} %param.21) | non-fusion elementwise | flops 192 | bytes 1152 | tf_op jit(solution)/shard_map/reshape | solution.py:292
  6.2 1.3 %reshape.63.b_in = f32[1,384]{1,0:T(1,128)} reshape(bf16[384]{0:T(512)(128)(2,1)} %param.13) | data formatting | bytes 2304 | tf_op jit(solution)/shard_map/reshape | solution.py:292
  7.4 1.2 %copy.15 = bf16[2,20,16,16]{3,2,1,0:T(8,128)(2,1)S(1)} copy(bf16[2,20,16,16]{1,3,2,0:T(8,128)(2,1)} %param.11) | data formatting | bytes 40960 | tf_op args[0]
  8.6 0.2 reshape.45
  8.8 0.6 pad.4.lat
  9.4 3.7 %copy.16 = bf16[3,3,384,192]{3,2,1,0:T(8,128)(2,1)} copy(bf16[3,3,384,192]{2,3,1,0:T(8,128)(2,1)} %param.14) | data formatting | bytes 2654208 | tf_op args[3]
  13.1 82.8 %shard_map.109 = bf16[2,4,320,192]{3,2,1,0:T(8,128)(2,1)} custom-call(bf16[48,256]{1,0:T(8,128)(2,1)} %pad.4.lat, bf16[3,144,384]{2,1,0:T(8,128)(2,1)} %bitcast.14, f32[1,384]{1,0:T(1,128)} %reshape.63.b_in, bf16[9,384,192]{2,1,0:T(8,128)(2,1)} %bitcast.11, f32[1,192]{1,0:T(1,128)} %bitcast.15, f32[1,192]{1,0:T(1,128)} %bitcast.16, ...), custom_call_target="tpu_custom_call" | custom-call | tf_op jit(solution)/shard_map/pallas_call | solution.py:298
  96.0 2.5 %copy.17 = bf16[2,4,320,192]{2,3,1,0:T(8,128)(2,1)} copy(bf16[2,4,320,192]{3,2,1,0:T(8,128)(2,1)} %shard_map.109) | data formatting | bytes 1966080 | tf_op jit(solution)/shard_map/pallas_call | solution.py:298
where the time goes:
time: 100 us; the launch traced here: 98.4 us
  Pallas kernels  82.8 us (83%)
  local copies, waits for them, and re-layouts  9.41 us (9%)
  other arithmetic  6.15 us (6%)
    pallas_call x1, Pallas kernels, per_device(): pl.pallas_call(functools.partial(kernel, ntm, nt, height, shard, zch), ou...  82.8 us
    reshape x5, other arithmetic, per_device(): vec = lambda v: v.astype(F32).reshape(1, -1)  6.15 us
    unnamed x2, local copies, waits for them, and re-layouts  4.88 us
    pallas_call x1, local copies, waits for them, and re-layouts, per_device(): pl.pallas_call(functools.partial(kernel, ntm, nt, height, shard, zch), ou...  2.47 us

commit v1 on v0

--- a/solution.py
+++ b/solution.py
@@ -16,6 +16,10 @@
     return jnp.dot(a, b, preferred_element_type=F32)
 
 
+def dot_t(a, b):
+    return lax.dot_general(a, b, (((1,), (1,)), ((), ())), preferred_element_type=F32)
+
+
 def activate(v, gain):
     v = v.astype(F32)
     inv = lax.rsqrt(jnp.mean(v * v, axis=-1, keepdims=True) + 1e-6)
@@ -35,8 +39,7 @@
 
 
 def kernel(ntm, nt, height, shard, zch,
-           lat, w_in, b_in, w_up, b_up, g_one, w_one, b_one, g_two, w_two, b_two,
-           out,
+           lat, w_in, w_up, w_one, w_two, vb_in, vb_up, vg_one, vb_one, vg_two, vb_two, out,
            lbuf, lf32, sel, cols, first, wc, plane, a1, a2, acc,
            lsend, lrecv, osend, hsend, arecv):
     tm = lax.axis_index("tm")
@@ -44,6 +47,10 @@
     ncol = nt * shard
     dim = first.shape[-1]
     upd = plane.shape[-1]
+
+    b_in, b_up, g_one, b_one, g_two, b_two = (
+        v[...].astype(F32).reshape(1, v.shape[0])
+        for v in (vb_in, vb_up, vg_one, vb_one, vg_two, vb_two))
 
     barrier = pltpu.get_barrier_semaphore()
 
@@ -86,7 +93,7 @@
         sel[:, 256 * r:256 * r + 256] = jnp.where(hit, 1.0, 0.0).astype(BF16)
 
     def phases(j, c):
-        at = pl.ds(pl.multiple_of(j * 64, 64), 64)
+        at = pl.ds(pl.multiple_of(j * 32, 32), 32)
         w = [[w_up[3 * p + q, at].astype(F32) for q in range(3)] for p in range(3)]
 
         def joined(v, phase):
@@ -102,7 +109,7 @@
                     for cc in range(2):
                         wc[2 * a + b, 2 * rr + cc, at] = both[cc].astype(BF16)
         return c
-    lax.fori_loop(0, dim // 64, phases, 0)
+    lax.fori_loop(0, upd // 32, phases, 0)
 
     for d in range(3):
         @pl.when(tm - d >= 0)
@@ -131,7 +138,7 @@
 
     def conv_in(k, c):
         f, r = k // 4, k % 4
-        v = b_in[...] + sum(dot(cols[f + a, r][:, :9 * zch], w_in[a]) for a in range(3))
+        v = b_in + sum(dot(cols[f + a, r][:, :9 * zch], w_in[a]) for a in range(3))
         row = 2 * tile - 1 + r
         keep = ((row >= 0) & (row < height)).astype(F32)
         v = v * keep
@@ -153,11 +160,11 @@
         seen = ((tm > 0) | (f >= 2))
         for a in range(2):
             for b in range(2):
-                v = b_up[...]
+                v = b_up
                 for rr in range(2):
                     for cc in range(2):
                         x = first[b + cc, f, rr:rr + 3].reshape(3 * ncol, dim)
-                        v = v + dot(x, wc[2 * a + b, 2 * rr + cc])
+                        v = v + dot_t(x, wc[2 * a + b, 2 * rr + cc])
                 v = v.astype(BF16)
                 for base in range(3):
                     row = 2 * base + 1 - a
@@ -168,7 +175,7 @@
                         ok = ok & (tile > 0)
                     if row == 5:
                         ok = ok & (tile < nt - 1)
-                    split_store(a1, (f, row), b, activate(here, g_one[...]) * ok.astype(F32))
+                    split_store(a1, (f, row), b, activate(here, g_one) * ok.astype(F32))
         return c
     lax.fori_loop(0, 4, conv_up, 0)
 
@@ -199,17 +206,18 @@
         def _():
             act(copy(f + 2, r + 1, f + 2, 5, 0, -1, hsend.at[f, 0, 0]))
 
-        @pl.when((r == 0) & (tile > 0) & (tm + 1 < ntm))
-        def _():
-            act(copy(f + 2, r + 1, f, 5, 1, -1, hsend.at[f, 0, 1]))
-
         @pl.when((r == 3) & (tile < nt - 1))
         def _():
             act(copy(f + 2, r + 1, f + 2, 0, 0, 1, hsend.at[f, 1, 0]))
 
-        @pl.when((r == 3) & (tile < nt - 1) & (tm + 1 < ntm))
-        def _():
-            act(copy(f + 2, r + 1, f, 0, 1, 1, hsend.at[f, 1, 1]))
+    def forwards(f, act):
+        @pl.when((tm > 0) & (tile > 0))
+        def _():
+            act(copy(f, 1, f, 5, 0, -1, hsend.at[f, 0, 1]))
+
+        @pl.when((tm > 0) & (tile < nt - 1))
+        def _():
+            act(copy(f, 4, f, 0, 0, 1, hsend.at[f, 1, 1]))
 
     def where_at(k):
         f = k % 2
@@ -218,18 +226,26 @@
 
     def conv_mid(k, c):
         f, r = where_at(k)
-        v = (conv_part(a1, w_one, f, r, (0, 1, 2)) + b_one[...]).astype(BF16)
-        v = activate(v, g_two[...])
+        v = (conv_part(a1, w_one, f, r, (0, 1, 2)) + b_one).astype(BF16)
+        v = activate(v, g_two)
         split_store(a2, (f + 2, r + 1), 0, v[:ncol])
         split_store(a2, (f + 2, r + 1), 1, v[ncol:])
         sends(f, r, lambda c: c.start())
         return c
     lax.fori_loop(0, 8, conv_mid, 0)
 
-    def receive(f, row, ok):
+    for f in (0, 1):
+        @pl.when(tm > 0)
+        def _():
+            for row in (1, 4):
+                copy(f, row, f, row, 0, 0, osend.at[0, 0]).wait_recv()
+        forwards(f, lambda c: c.start())
+
+    def receive(f, row, ok, wait=True):
         @pl.when(ok)
         def _():
-            copy(f, row, f, row, 0, 0, osend.at[0, 0]).wait_recv()
+            if wait:
+                copy(f, row, f, row, 0, 0, osend.at[0, 0]).wait_recv()
             a2[f, row, 3 * ncol:] = ahead(a2[f, row, ncol:2 * ncol].astype(F32)).astype(BF16)
             a2[f, row, :ncol] = after(a2[f, row, 2 * ncol:3 * ncol].astype(F32)).astype(BF16)
 
@@ -248,23 +264,21 @@
     lax.fori_loop(0, 4, conv_near, 0)
 
     for f in (0, 1):
+        for row in (1, 2, 3, 4):
+            receive(f, row, tm > 0, row in (2, 3))
         receive(f, 0, (tm > 0) & (tile > 0))
         receive(f, 5, (tm > 0) & (tile < nt - 1))
 
-        def middle_rows(row, c):
-            receive(f, row, tm > 0)
-            return c
-        lax.fori_loop(1, 5, middle_rows, 0)
-
     m = lax.broadcasted_iota(jnp.int32, (2 * ncol, 2 * ncol), 0)
     n = lax.broadcasted_iota(jnp.int32, (2 * ncol, 2 * ncol), 1)
-    weave = jnp.where(n == (m % 2) * ncol + m // 2, 1.0, 0.0).astype(BF16)
+    weave = jnp.where(m == (n % 2) * ncol + n // 2, 1.0, 0.0).astype(BF16)
 
     def conv_far(r, c):
         for f, kts in ((0, (0, 1)), (1, (0,))):
-            v = acc[f, r] + conv_part(a2, w_two, f, r, kts) + b_two[...]
+            v = acc[f, r] + conv_part(a2, w_two, f, r, kts) + b_two
             v = (v + plane[f + 2, r + 1].astype(F32)).astype(BF16)
-            out[f, r] = dot(weave, v).astype(BF16)
+            out[f, r] = lax.dot_general(
+                v, weave, (((0,), (0,)), ((), ())), preferred_element_type=F32).astype(BF16)
         return c
     lax.fori_loop(0, 4, conv_far, 0)
 
@@ -278,6 +292,8 @@
         sends(f, r, lambda c: c.wait_send())
         return c
     lax.fori_loop(0, 8, left, 0)
+    for f in (0, 1):
+        forwards(f, lambda c: c.wait_send())
 
 
 def per_device(latents, w_in, b_in, w_up, b_up, gain_one, w_one, b_one, gain_two, w_two, b_two):
@@ -289,15 +305,14 @@
     deep = -(-frames * shard // 16) * 16
     lat = jnp.pad(lat, ((0, deep - frames * shard), (0, 0)))
     wide = height * zch
-    vec = lambda v: v.astype(F32).reshape(1, -1)
-    args = (lat, w_in.reshape(3, 9 * zch, dim), vec(b_in), w_up.reshape(9, dim, upd), vec(b_up),
-            vec(gain_one), w_one.reshape(27, upd, upd), vec(b_one), vec(gain_two),
-            w_two.reshape(27, upd, upd), vec(b_two))
+    args = (lat, w_in.reshape(3, 9 * zch, dim),
+            jnp.swapaxes(w_up, 2, 3).reshape(9, upd, dim), w_one.reshape(27, upd, upd),
+            w_two.reshape(27, upd, upd), b_in, b_up, gain_one, b_one, gain_two, b_two)
     vmem = pl.BlockSpec(memory_space=pltpu.VMEM)
     dma = pltpu.SemaphoreType.DMA
-    return pl.pallas_call(
+    decoded = pl.pallas_call(
         functools.partial(kernel, ntm, nt, height, shard, zch),
-        out_shape=jax.ShapeDtypeStruct((frames, 4, 2 * ncol, upd), BF16),
+        out_shape=jax.ShapeDtypeStruct((frames, 4, upd, 2 * ncol), BF16),
         in_specs=[vmem] * len(args),
         out_specs=vmem,
         scratch_shapes=[
@@ -306,7 +321,7 @@
             pltpu.VMEM((wide, 1024), BF16),
             pltpu.VMEM((6, 4, ncol, 256), BF16),
             pltpu.VMEM((3, 4, 4, ncol, dim), BF16),
-            pltpu.VMEM((4, 4, dim, upd), BF16),
+            pltpu.VMEM((4, 4, upd, dim), BF16),
             pltpu.VMEM((4, 6, 2 * ncol, upd), BF16),
             pltpu.VMEM((4, 6, 4 * ncol, upd), BF16),
             pltpu.VMEM((4, 6, 4 * ncol, upd), BF16),
@@ -320,6 +335,7 @@
         compiler_params=pltpu.CompilerParams(
             collective_id=0, has_side_effects=True, vmem_limit_bytes=60 * 2**20),
     )(*args)
+    return jnp.swapaxes(decoded, 2, 3)
 
 
 def solution(mesh):

time: 100 us -> 86.7 us (0.87); the launches traced: 98.4 us -> 86.5 us
  other arithmetic: 6.15 us -> 0 us
  local copies, waits for them, and re-layouts: 9.41 us -> 4.42 us
    reshape x5 -> x0, other arithmetic: 6.15 us -> none  [per_device(): vec = lambda v: v.astype(F32).reshape(1, -1)]
    pallas_call x1 -> x0, local copies, waits for them, and re-layouts: 2.47 us -> none  [per_device(): pl.pallas_call(functools.partial(kernel, ntm, nt, height, shard, zch), ou...]
    unnamed x2, local copies, waits for them, and re-layouts: 4.88 us -> 3.62 us
    reshape x1 -> x0, local copies, waits for them, and re-layouts: 1.25 us -> none  [per_device(): vec = lambda v: v.astype(F32).reshape(1, -1)]
where the time goes in v1:
time: 86.7 us; the launch traced here: 86.5 us
  Pallas kernels  82.1 us (95%)
  local copies, waits for them, and re-layouts  4.42 us (5%)
    pallas_call x1, Pallas kernels, per_device(): pl.pallas_call(functools.partial(kernel, ntm, nt, height, shard, zch), ou...  82.1 us
    unnamed x2, local copies, waits for them, and re-layouts  3.62 us

profile of v1, /device:TPU:8, one launch (start us, length us, event | category | flops | bytes accessed | tf_op | source)
XLA Modules:
  0.0 86.5 jit_solution(4845633228705980751)
XLA Ops:
  0.0 1.2 %copy.13 = bf16[2,20,16,16]{3,2,1,0:T(8,128)(2,1)S(1)} copy(bf16[2,20,16,16]{1,3,2,0:T(8,128)(2,1)} %param.11) | data formatting | bytes 40960 | tf_op args[0]
  1.2 0.2 reshape.15
  1.4 0.6 pad.4.lat
  2.0 82.1 %shard_map.109 = bf16[2,4,192,320]{3,2,1,0:T(8,128)(2,1)} custom-call(bf16[48,256]{1,0:T(8,128)(2,1)} %pad.4.lat, bf16[3,144,384]{2,1,0:T(8,128)(2,1)} %bitcast.13, bf16[9,192,384]{2,1,0:T(8,128)(2,1)} %bitcast.12, bf16[27,192,192]{2,1,0:T(8,128)(2,1)} %bitcast.10, bf16[27,192,192]{2,1,0:T(8,128)(2,1)} %bitcast.11, bf16[384]{0:T(512)(128)(2,1)} %vb_in.1, ...), custom_call_target="tpu_custom_call" | custom-call | tf_op jit(solution)/shard_map/pallas_call | solution.py:313
  84.1 2.4 %copy.15 = bf16[2,4,320,192]{2,3,1,0:T(8,128)(2,1)} copy(bf16[2,4,320,192]{2,3,1,0:T(8,128)(2,1)} %bitcast.9) | data formatting | bytes 1966080

commit v2 on v1

--- a/solution.py
+++ b/solution.py
@@ -39,9 +39,9 @@
 
 
 def kernel(ntm, nt, height, shard, zch,
-           lat, w_in, w_up, w_one, w_two, vb_in, vb_up, vg_one, vb_one, vg_two, vb_two, out,
+           lat, w_in, w_up, far_one, far_two, vb_in, vb_up, vg_one, vb_one, vg_two, vb_two, out,
            lbuf, lf32, sel, cols, first, wc, plane, a1, a2, acc,
-           lsend, lrecv, osend, hsend, arecv):
+           lsend, lrecv, osend, hsend, arecv, w_one, w_two, wsem):
     tm = lax.axis_index("tm")
     tile = lax.axis_index("tile")
     ncol = nt * shard
@@ -51,6 +51,11 @@
     b_in, b_up, g_one, b_one, g_two, b_two = (
         v[...].astype(F32).reshape(1, v.shape[0])
         for v in (vb_in, vb_up, vg_one, vb_one, vg_two, vb_two))
+
+    fetch_one = pltpu.make_async_copy(far_one, w_one, wsem.at[0])
+    fetch_two = pltpu.make_async_copy(far_two, w_two, wsem.at[1])
+    fetch_one.start()
+    fetch_two.start()
 
     barrier = pltpu.get_barrier_semaphore()
 
@@ -232,6 +237,8 @@
         split_store(a2, (f + 2, r + 1), 1, v[ncol:])
         sends(f, r, lambda c: c.start())
         return c
+    fetch_one.wait()
+    fetch_two.wait()
     lax.fori_loop(0, 8, conv_mid, 0)
 
     for f in (0, 1):
@@ -313,7 +320,7 @@
     decoded = pl.pallas_call(
         functools.partial(kernel, ntm, nt, height, shard, zch),
         out_shape=jax.ShapeDtypeStruct((frames, 4, upd, 2 * ncol), BF16),
-        in_specs=[vmem] * len(args),
+        in_specs=[vmem] * 3 + [pl.BlockSpec(memory_space=pl.ANY)] * 2 + [vmem] * 6,
         out_specs=vmem,
         scratch_shapes=[
             pltpu.VMEM((3, nt, deep, wide), BF16),
@@ -331,6 +338,9 @@
             dma((2, 4)),
             dma((2, 2, 2)),
             dma((4, 6)),
+            pltpu.VMEM((27, upd, upd), BF16),
+            pltpu.VMEM((27, upd, upd), BF16),
+            dma((2,)),
         ],
         compiler_params=pltpu.CompilerParams(
             collective_id=0, has_side_effects=True, vmem_limit_bytes=60 * 2**20),

time: 86.7 us -> 85.1 us (0.982)
  Pallas kernels: 82.1 us -> 80.5 us
    pallas_call x1, Pallas kernels: 82.1 us -> 80.5 us  [per_device(): pl.pallas_call(functools.partial(kernel, ntm, nt, height, shard, zch), ou...]
where the time goes in v2:
time: 85.1 us; the launch traced here: 84.9 us
  Pallas kernels  80.5 us (95%)
  local copies, waits for them, and re-layouts  4.42 us (5%)
    pallas_call x1, Pallas kernels, per_device(): pl.pallas_call(functools.partial(kernel, ntm, nt, height, shard, zch), ou...  80.5 us
    unnamed x2, local copies, waits for them, and re-layouts  3.62 us

profile of v2, /device:TPU:8, one launch (start us, length us, event | category | flops | bytes accessed | tf_op | source)
XLA Modules:
  0.0 84.9 jit_solution(11839627109156121348)
XLA Ops:
  0.0 1.2 %copy.13 = bf16[2,20,16,16]{3,2,1,0:T(8,128)(2,1)S(1)} copy(bf16[2,20,16,16]{1,3,2,0:T(8,128)(2,1)} %param.11) | data formatting | bytes 40960 | tf_op args[0]
  1.2 0.2 reshape.15
  1.4 0.6 pad.4.lat
  2.0 80.5 %shard_map.109 = bf16[2,4,192,320]{3,2,1,0:T(8,128)(2,1)} custom-call(bf16[48,256]{1,0:T(8,128)(2,1)} %pad.4.lat, bf16[3,144,384]{2,1,0:T(8,128)(2,1)} %bitcast.13, bf16[9,192,384]{2,1,0:T(8,128)(2,1)} %bitcast.12, bf16[27,192,192]{2,1,0:T(8,128)(2,1)} %bitcast.10, bf16[27,192,192]{2,1,0:T(8,128)(2,1)} %bitcast.11, bf16[384]{0:T(512)(128)(2,1)} %vb_in.1, ...), custom_call_target="tpu_custom_call" | custom-call | tf_op jit(solution)/shard_map/pallas_call | solution.py:320
  82.5 2.4 %copy.15 = bf16[2,4,320,192]{2,3,1,0:T(8,128)(2,1)} copy(bf16[2,4,320,192]{2,3,1,0:T(8,128)(2,1)} %bitcast.9) | data formatting | bytes 1966080
